TPU v7x, 32 devices: a whole 2x2x4 slice. The times are simulated.
32 devices in a mesh: groups: 2 (over y), fsdp: 4 (over z), owner: 4 (over x, core).
Axes of the slice: x: 2, y: 2, z: 4, core: 2. Of those that a mesh axis runs over, the one named last changes fastest.
Arguments:
- inputs: bfloat16 [13312, 8192], P(('groups', 'fsdp'), 'owner'), parts along dimension 0, may hold values from -6 to 6
- value_matrix: bfloat16 [1024, 8192], P('fsdp', 'owner'), may hold values from -0.0625 to 0.0625
- adapter_down_weight: float32 [8, 64, 8192], P(('groups', 'fsdp'), None, 'owner'), parts along dimension 0, may hold values from -6 to 6
- adapter_up_weight: float32 [8, 64, 1024], P(('groups', 'fsdp'), None, 'owner'), parts along dimension 0, may hold values from -6 to 6
- down_first_moment: float32 [8, 64, 8192], P(('groups', 'fsdp'), None, 'owner'), parts along dimension 0, may hold values from -2 to 2
- down_second_moment: float32 [8, 64, 8192], P(('groups', 'fsdp'), None, 'owner'), parts along dimension 0, may hold values from 0.05 to 2
- up_first_moment: float32 [8, 64, 1024], P(('groups', 'fsdp'), None, 'owner'), parts along dimension 0, may hold values from -2 to 2
- up_second_moment: float32 [8, 64, 1024], P(('groups', 'fsdp'), None, 'owner'), parts along dimension 0, may hold values from 0.05 to 2
- output_gradient: bfloat16 [13312, 1024], P(('groups', 'fsdp'), 'owner'), parts along dimension 0, may hold values from -6 to 6
- tenant_of_block: int32 [104], P('groups'), parts along dimension 0, may hold values from 0 to 3, as said below
- tenant_storage_slot: int32 [8], P('groups'), parts along dimension 0, may hold values from 0 to 3, as said below
Outputs:
- values: bfloat16 [13312, 1024], P(('groups', 'fsdp'), 'owner'), parts along dimension 0
- updated_down_weight: float32 [8, 64, 8192], P(('groups', 'fsdp'), None, 'owner'), parts along dimension 0
- updated_up_weight: float32 [8, 64, 1024], P(('groups', 'fsdp'), None, 'owner'), parts along dimension 0
- updated_down_first: float32 [8, 64, 8192], P(('groups', 'fsdp'), None, 'owner'), parts along dimension 0
- updated_down_second: float32 [8, 64, 8192], P(('groups', 'fsdp'), None, 'owner'), parts along dimension 0
- updated_up_first: float32 [8, 64, 1024], P(('groups', 'fsdp'), None, 'owner'), parts along dimension 0
- updated_up_second: float32 [8, 64, 1024], P(('groups', 'fsdp'), None, 'owner'), parts along dimension 0
There are 2 independent parts, one for each index of `groups`. A program takes and returns all parts, laid end to end along the dimension named above; an argument that names none is the same for every part. Nothing has to cross between parts.
Inputs may be any that keep to these rules, and one draw needn't show every extreme that they name: `tenant_storage_slot`: A permutation of the slots. Slot s is stored on index s of fsdp. `tenant_of_block`: the 13 blocks of one bin use at most one slot stored on each fsdp index; the first min(13, 4) blocks of a bin lie on distinct fsdp indices, and block b + 4 of a bin has the tenant of block b.
All inputs are finite; a program needn't handle non-finite values.
Results may differ from a plain program's by a relative error of at most 0.0045.
Values may be sent and summed in bfloat16 or wider, within the bound.
A program may use at most 128 MiB of HBM per device.

v0:
```python
import math

import jax
import jax.numpy as jnp
from jax import lax
from jax.sharding import PartitionSpec as P

MODEL_WIDTH = 8192
BLOCK = 128


branch_scale = 0.5
first_moment = 0.9
second_moment = 0.999
learning_rate = 0.05
decay_rate = 0.01
epsilon = 1e-08
first_correction = 1.0 - math.exp(100.0 * math.log(0.9))
second_correction = 1.0 - math.exp(100.0 * math.log(0.999))


def adam_weight_update(weights, moment, second, gradient):
    new_moment = first_moment * moment + (1.0 - first_moment) * gradient
    new_second = second_moment * second + (1.0 - second_moment) * gradient * gradient
    direction = new_moment / first_correction / (jnp.sqrt(new_second / second_correction) + epsilon)
    new_weights = weights - learning_rate * (direction + decay_rate * weights)
    return (new_weights, new_moment, new_second)


def base_product(inputs, value_matrix):
    return jnp.einsum(
        "tk,jk->tj",
        inputs,
        lax.all_gather(value_matrix, "fsdp", axis=0, tiled=True),
        preferred_element_type=jnp.float32,
    )


def finish_values(base_values, low, block_up, up_factor):
    low_half = low.astype(jnp.bfloat16)
    extra = (
        jnp.einsum("brt,brj->btj", low_half, block_up, preferred_element_type=jnp.float32)
        * up_factor
    )
    return (low_half, (base_values + extra.reshape(base_values.shape)).astype(jnp.bfloat16))


def per_device(
    inputs,
    value_matrix,
    adapter_down_weight,
    adapter_up_weight,
    down_first_moment,
    down_second_moment,
    up_first_moment,
    up_second_moment,
    output_gradient,
    tenant_of_block,
    tenant_storage_slot,
):
    highest = lax.Precision.HIGHEST
    bin_count = lax.axis_size("fsdp")
    my_index = lax.axis_index("fsdp")
    tok_rows, quarter = inputs.shape
    block_count = tok_rows // BLOCK
    per_worker_share = adapter_down_weight.shape[0]
    adapter_rank_size = adapter_down_weight.shape[1]
    column_portion = adapter_up_weight.shape[2]
    adapter_count = tenant_storage_slot.shape[0]
    tenant_ids = jnp.arange(adapter_count, dtype=jnp.int32)
    slot_of_block = jnp.sum(
        jnp.where(tenant_of_block[:, None] == tenant_ids[None, :], tenant_storage_slot[None, :], 0),
        axis=1,
    )
    slot_grid = slot_of_block.reshape(bin_count, block_count)
    owner_grid = slot_grid // per_worker_share
    local_grid = slot_grid % per_worker_share
    local_ids = jnp.arange(per_worker_share, dtype=jnp.int32)
    wanted = jnp.any(
        (owner_grid[:, :, None] == my_index) & (local_grid[:, :, None] == local_ids[None, None, :]),
        axis=1,
    )
    chosen = wanted.astype(jnp.bfloat16)
    down_portion = adapter_down_weight.astype(jnp.bfloat16)
    up_portion = adapter_up_weight.astype(jnp.bfloat16)
    my_owners = lax.dynamic_index_in_dim(owner_grid, my_index, 0, keepdims=False)
    partial_value = base_product(inputs, value_matrix)
    send_down = jnp.einsum(
        "fj,jrk->frk", chosen, down_portion, preferred_element_type=jnp.float32
    ).astype(jnp.bfloat16)
    send_up = jnp.einsum(
        "fj,jrk->frk", chosen, up_portion, preferred_element_type=jnp.float32
    ).astype(jnp.bfloat16)
    arrived_down, arrived_up = (
        lax.all_to_all(send_down, "fsdp", split_axis=0, concat_axis=0, tiled=True),
        lax.all_to_all(send_up, "fsdp", split_axis=0, concat_axis=0, tiled=True),
    )
    block_down = jnp.take(arrived_down, my_owners, axis=0)
    block_up = jnp.take(arrived_up, my_owners, axis=0)
    row_blocks = inputs.reshape(block_count, BLOCK, quarter)
    grad_blocks = output_gradient.reshape(block_count, BLOCK, column_portion)
    down_factor = 1.0 / math.sqrt(MODEL_WIDTH)
    up_factor = branch_scale / math.sqrt(adapter_rank_size)
    low_part = (
        jnp.einsum("brk,btk->brt", block_down, row_blocks, preferred_element_type=jnp.float32)
        * down_factor
    )
    back_part = (
        jnp.einsum("btj,brj->brt", grad_blocks, block_up, preferred_element_type=jnp.float32)
        * up_factor
    )
    base_values = lax.psum_scatter(partial_value, "owner", scatter_dimension=1, tiled=True)
    low = lax.psum(low_part, "owner")
    low_half, values = finish_values(base_values, low, block_up, up_factor)
    back = lax.psum(back_part.astype(jnp.bfloat16), "owner")
    up_blocks = (
        jnp.einsum("brt,btj->brj", low_half, grad_blocks, preferred_element_type=jnp.float32)
        * up_factor
    )
    down_blocks = (
        jnp.einsum("brt,btk->brk", back, row_blocks, preferred_element_type=jnp.float32)
        * down_factor
    )
    route = (my_owners[:, None] == jnp.arange(bin_count, dtype=jnp.int32)[None, :]).astype(
        jnp.float32
    )
    back_down = jnp.einsum("bg,brk->grk", route, down_blocks, precision=highest).astype(
        jnp.bfloat16
    )
    back_up = jnp.einsum("bg,brj->grj", route, up_blocks, precision=highest).astype(jnp.bfloat16)
    returned_down, returned_up = (
        lax.all_to_all(back_down, "fsdp", split_axis=0, concat_axis=0, tiled=True),
        lax.all_to_all(back_up, "fsdp", split_axis=0, concat_axis=0, tiled=True),
    )
    down_gradient = jnp.einsum(
        "fj,frk->jrk", chosen, returned_down, preferred_element_type=jnp.float32
    )
    up_gradient = jnp.einsum("fj,frk->jrk", chosen, returned_up, preferred_element_type=jnp.float32)
    updated_down_weight, updated_down_first, updated_down_second = adam_weight_update(
        adapter_down_weight, down_first_moment, down_second_moment, down_gradient
    )
    updated_up_weight, updated_up_first, updated_up_second = adam_weight_update(
        adapter_up_weight, up_first_moment, up_second_moment, up_gradient
    )
    return (
        values,
        updated_down_weight,
        updated_up_weight,
        updated_down_first,
        updated_down_second,
        updated_up_first,
        updated_up_second,
    )


def solution(mesh):
    in_specs = (
        P(("groups", "fsdp"), "owner"),
        P("fsdp", "owner"),
        P(("groups", "fsdp"), None, "owner"),
        P(("groups", "fsdp"), None, "owner"),
        P(("groups", "fsdp"), None, "owner"),
        P(("groups", "fsdp"), None, "owner"),
        P(("groups", "fsdp"), None, "owner"),
        P(("groups", "fsdp"), None, "owner"),
        P(("groups", "fsdp"), "owner"),
        P("groups"),
        P("groups"),
    )
    out_specs = (
        P(("groups", "fsdp"), "owner"),
        P(("groups", "fsdp"), None, "owner"),
        P(("groups", "fsdp"), None, "owner"),
        P(("groups", "fsdp"), None, "owner"),
        P(("groups", "fsdp"), None, "owner"),
        P(("groups", "fsdp"), None, "owner"),
        P(("groups", "fsdp"), None, "owner"),
    )
    return jax.shard_map(
        per_device, mesh=mesh, in_specs=in_specs, out_specs=out_specs, check_vma=False
    )
```

profile of v0, /device:TPU:0, one launch (start us, length us, event | category | flops | bytes accessed | tf_op | source)
XLA Modules:
  0.0 224.8 jit_solution(14514606990301661661)
XLA Ops:
  8.1 0.7 all-gather.2.cloned.1.call-update
  8.8 0.8 select_reduce_fusion
  9.5 0.1 eq.57
  9.6 0.1 reduce_or.9
  9.7 0.8 bitcast_convert_fusion.1
  10.6 0.7 multiply_convert_fusion.1
  11.3 6.3 %all-to-all-start.1 = ((bf16[4,64,256]{2,1,0:T(8,128)(2,1)}), bf16[4,64,256]{2,1,0:T(8,128)(2,1)S(1)}, u32[]{:S(2)}, u32[]{:S(2)}) async-start(bf16[4,64,256]{2,1,0:T(8,128)(2,1)} %multiply_convert_fusion.1), calls=%async_computation.2 | async-start | bytes 262144 | tf_op jit(solution)/shard_map/all_to_all | solution.py:96
  17.8 5.9 %all-to-all-done.1 = bf16[4,64,256]{2,1,0:T(8,128)(2,1)S(1)} async-done(((bf16[4,64,256]{2,1,0:T(8,128)(2,1)}), bf16[4,64,256]{2,1,0:T(8,128)(2,1)S(1)}, u32[]{:S(2)}, u32[]{:S(2)}) %all-to-all-start.1) | async-done | bytes 131104 | tf_op jit(solution)/shard_map/all_to_all | solution.py:96
  23.7 0.6 gather_fusion.1
  24.3 1.2 fusion.10
  25.5 68.5 %all-gather.2.cloned.1.call-done = bf16[1024,2048]{1,0:T(8,128)(2,1)} async-done(((bf16[256,2048]{1,0:T(8,128)(2,1)}), bf16[1024,2048]{1,0:T(8,128)(2,1)}) %all-gather.2.cloned.1.call-update) | async-done | bytes 4194320 | tf_op jit(solution)/shard_map/all_gather | solution.py:34
  94.0 12.4 %fusion.38 = f32[1664,1024]{1,0:T(8,128)} fusion(bf16[1664,2048]{1,0:T(8,128)(2,1)} %param.11, bf16[1024,2048]{1,0:T(8,128)(2,1)} %all-gather.2.cloned.1.call-done), kind=kOutput, calls=%fused_computation.62 | convolution fusion | flops 6979321856 | bytes 17825792 | tf_op jit(solution)/shard_map/tk,jk->tj/dot_general | solution.py:31
  106.5 4.3 %convolution_multiply_fusion = f32[13,64,2048]{2,1,0:T(8,128)S(1)} fusion(bf16[13,64,128]{2,1,0:T(8,128)(2,1)} %all-reduce.3.cloned.1.call-done, bf16[13,128,2048]{2,1,0:T(8,128)(2,1)} %bitcast.70), kind=kOutput, calls=%fused_computation.4 | convolution fusion | flops 437911552 | bytes 13844480 | tf_op jit(solution)/shard_map/brt,btk->brk/dot_general | solution.py:121
  110.8 7.6 %fusion = bf16[4,64,2048]{2,0,1:T(4,128)(2,1)S(1)} fusion(f32[13,64,2048]{2,1,0:T(8,128)S(1)} %convolution_multiply_fusion, s32[13]{0:T(128)S(1)} %get-tuple-element.14), kind=kOutput, calls=%fused_computation.2 | convolution fusion | flops 81788976 | bytes 7864372 | tf_op jit(solution)/shard_map/bg,brk->grk/dot_general | solution.py:127
  118.5 0.6 copy.40
  119.0 28.4 %all_to_all.20 = bf16[4,64,2048]{2,1,0:T(8,128)(2,1)S(1)} all-to-all(bf16[4,64,2048]{2,1,0:T(8,128)(2,1)S(1)} %copy.40), channel_id=1, replica_groups=mesh['groups'=2,'fsdp'=4,'owner'=4] {'fsdp'}, dimensions={0} | all-to-all | bytes 2097152 | tf_op jit(solution)/shard_map/all_to_all | solution.py:132
  147.5 0.9 fusion.13
  148.4 1.6 multiply_subtract_fusion
  150.0 0.2 multiply_convert_fusion
  150.2 27.8 %all_to_all.21 = bf16[4,64,2048]{2,1,0:T(8,128)(2,1)S(1)} all-to-all(bf16[4,64,2048]{2,1,0:T(8,128)(2,1)S(1)} %multiply_convert_fusion), channel_id=1, replica_groups=mesh['groups'=2,'fsdp'=4,'owner'=4] {'fsdp'}, dimensions={0} | all-to-all | bytes 2097152 | tf_op jit(solution)/shard_map/all_to_all | solution.py:95
  178.0 2.6 %gather_fusion = bf16[13,64,2048]{2,1,0:T(8,128)(2,1)} fusion(bf16[4,64,2048]{2,1,0:T(8,128)(2,1)S(1)} %all_to_all.21, s32[1024]{0:T(1024)S(1)} %pad_clamp_fusion), kind=kCustom, calls=%fused_computation | custom fusion | bytes 6815796 | tf_op jit(solution)/shard_map/jit(_take)/gather | solution.py:98
  180.6 6.5 %fusion.7 = f32[13,64,128]{2,1,0:T(8,128)S(1)} fusion(bf16[13,128,2048]{2,1,0:T(8,128)(2,1)} %bitcast.71, bf16[13,64,2048]{2,1,0:T(8,128)(2,1)} %gather_fusion, pred[13]{0:T(512)(128)(4,1)S(1)} %get-tuple-element.13), kind=kOutput, calls=%fused_computation.16 | convolution fusion | flops 438018048 | bytes 10649613 | tf_op jit(solution)/shard_map/brk,btk->brt/dot_general | solution.py:105
  187.1 15.0 %all-reduce.4 = bf16[13,64,128]{2,1,0:T(8,128)(2,1)S(1)} all-reduce(f32[13,64,128]{2,1,0:T(8,128)S(1)} %fusion.7), channel_id=1, replica_groups=mesh['groups'=2,'fsdp'=4,'owner'=4] {'owner'}, use_global_device_ids=true, to_apply=%region_3.4 | all-reduce | flops 106496 | bytes 638976 | tf_op jit(solution)/shard_map/psum | solution.py:113
  202.2 0.3 convolution_multiply_fusion.2
  202.4 1.0 fusion.11
  203.5 0.7 copy.41
  204.1 3.3 %all-to-all-start.3 = ((bf16[4,64,256]{2,1,0:T(8,128)(2,1)}), bf16[4,64,256]{2,1,0:T(8,128)(2,1)S(1)}, u32[]{:S(2)}, u32[]{:S(2)}) async-start(bf16[4,64,256]{2,1,0:T(8,128)(2,1)} %copy.41), calls=%async_computation.4 | async-start | bytes 262144 | tf_op jit(solution)/shard_map/all_to_all | solution.py:133
  207.5 0.5 convolution_multiply_fusion.1
  207.9 5.9 %all-to-all-done.3 = bf16[4,64,256]{2,1,0:T(8,128)(2,1)S(1)} async-done(((bf16[4,64,256]{2,1,0:T(8,128)(2,1)}), bf16[4,64,256]{2,1,0:T(8,128)(2,1)S(1)}, u32[]{:S(2)}, u32[]{:S(2)}) %all-to-all-start.3) | async-done | bytes 131104 | tf_op jit(solution)/shard_map/all_to_all | solution.py:133
  213.9 0.2 fusion.17
  214.1 0.7 multiply_subtract_fusion.1
  214.8 2.6 %fusion.5 = bf16[1664,256]{1,0:T(8,128)(2,1)} fusion(f32[1664,256]{1,0:T(8,128)} %reduce-scatter.2.cloned.1.call-done, f32[13,128,256]{2,1,0:T(8,128)S(1)} %convolution_multiply_fusion.1), kind=kLoop, calls=%fused_computation.11 | loop fusion | flops 851968 | bytes 4259840 | tf_op jit(solution)/shard_map/convert_element_type | solution.py:45
  (27 shorter events, 0.3 us)
Async XLA Ops:
  8.0 16.3 %copy-start = (bf16[1664,256]{1,0:T(8,128)(2,1)S(1)}, bf16[1664,256]{1,0:T(8,128)(2,1)}, u32[]{:S(2)}) copy-start(bf16[1664,256]{1,0:T(8,128)(2,1)} %param.19) | copy-start | bytes 2555908
  8.0 86.0 %all-gather.2.cloned.1.call-start = ((), (), s32[]{:S(2)}) async-start(), calls=%async_computation.5 | async-start | bytes 5242880 | tf_op jit(solution)/shard_map/all_gather | solution.py:34
  11.3 12.4 %all-to-all-start.1 = ((bf16[4,64,256]{2,1,0:T(8,128)(2,1)}), bf16[4,64,256]{2,1,0:T(8,128)(2,1)S(1)}, u32[]{:S(2)}, u32[]{:S(2)}) async-start(bf16[4,64,256]{2,1,0:T(8,128)(2,1)} %multiply_convert_fusion.1), calls=%async_computation.2 | async-start | bytes 262144 | tf_op jit(solution)/shard_map/all_to_all | solution.py:96
  17.6 88.8 %all-reduce.3.cloned.1.call-start = ((), (), s32[]{:S(2)}) async-start(), calls=%async_computation.7 | async-start | bytes 425984 | tf_op jit(solution)/shard_map/psum | solution.py:115
  25.5 189.3 %reduce-scatter.2.cloned.1.call-start = ((), (), s32[]{:S(2)}) async-start(), calls=%async_computation.6 | async-start | bytes 8519680 | tf_op jit(solution)/shard_map/reduce_scatter | solution.py:112
  118.4 29.9 %copy-start.1 = (f32[1,64,2048]{2,1,0:T(8,128)S(1)}, f32[1,64,2048]{2,1,0:T(8,128)}, u32[]{:S(2)}) copy-start(f32[1,64,2048]{2,1,0:T(8,128)} %param.13) | copy-start | bytes 1572868
  118.4 29.9 %copy-start.2 = (f32[1,64,2048]{2,1,0:T(8,128)S(1)}, f32[1,64,2048]{2,1,0:T(8,128)}, u32[]{:S(2)}) copy-start(f32[1,64,2048]{2,1,0:T(8,128)} %param.15) | copy-start | bytes 1572868
  118.4 29.9 %copy-start.3 = (f32[1,64,2048]{2,1,0:T(8,128)S(1)}, f32[1,64,2048]{2,1,0:T(8,128)}, u32[]{:S(2)}) copy-start(f32[1,64,2048]{2,1,0:T(8,128)} %param.16) | copy-start | bytes 1572868
  187.1 27.0 %copy-start.4 = (f32[1,64,256]{2,1,0:T(8,128)S(1)}, f32[1,64,256]{2,1,0:T(8,128)}, u32[]{:S(2)}) copy-start(f32[1,64,256]{2,1,0:T(8,128)} %param.14) | copy-start | bytes 196612
  187.1 27.0 %copy-start.5 = (f32[1,64,256]{2,1,0:T(8,128)S(1)}, f32[1,64,256]{2,1,0:T(8,128)}, u32[]{:S(2)}) copy-start(f32[1,64,256]{2,1,0:T(8,128)} %param.17) | copy-start | bytes 196612
  187.1 27.0 %copy-start.6 = (f32[1,64,256]{2,1,0:T(8,128)S(1)}, f32[1,64,256]{2,1,0:T(8,128)}, u32[]{:S(2)}) copy-start(f32[1,64,256]{2,1,0:T(8,128)} %param.18) | copy-start | bytes 196612
  204.1 9.7 %all-to-all-start.3 = ((bf16[4,64,256]{2,1,0:T(8,128)(2,1)}), bf16[4,64,256]{2,1,0:T(8,128)(2,1)S(1)}, u32[]{:S(2)}, u32[]{:S(2)}) async-start(bf16[4,64,256]{2,1,0:T(8,128)(2,1)} %copy.41), calls=%async_computation.4 | async-start | bytes 262144 | tf_op jit(solution)/shard_map/all_to_all | solution.py:133
Sparse Core Ops, SparseCore 0:
  10.5 83.4 all-gather.1
Sparse Core Ops, SparseCore 1:
  25.6 30.2 all-reduce.2
  106.5 60.3 reduce-scatter.1
where the time goes:
time: 225 us
  waiting for transfers between devices  81.1 us (36%)
  blocking collectives  71.3 us (32%)
  matrix products  34.8 us (15%)
  between operations  15.7 us (7%)
  starting transfers between devices  9.73 us (4%)
  other arithmetic  7.57 us (3%)
  local copies, waits for them, and re-layouts  4.66 us (2%)
    all_gather x1, waiting for transfers between devices, base_product(): lax.all_gather(value_matrix, 'fsdp', axis=0, tiled=True)  68.5 us
    all_to_all x1, blocking collectives, per_device(): lax.all_to_all(back_down, 'fsdp', split_axis=0, concat_axis=0, tiled=True)  28.4 us
    all_to_all x1, blocking collectives, per_device(): lax.all_to_all(send_down, 'fsdp', split_axis=0, concat_axis=0, tiled=True)  27.8 us
    psum x1, blocking collectives, per_device(): low = lax.psum(low_part, 'owner')  15 us
    dot_general x1, matrix products, base_product(): jnp.einsum('tk,jk->tj', inputs, lax.all_gather(value_matrix, 'fsdp', axis...  12.4 us
    dot_general x1, matrix products, per_device(): jnp.einsum('bg,brk->grk', route, down_blocks, precision=highest)  7.57 us
    dot_general x1, matrix products, per_device(): jnp.einsum('brk,btk->brt', block_down, row_blocks, preferred_element_type...  6.46 us
    all_to_all x1, starting transfers between devices, per_device(): lax.all_to_all(send_up, 'fsdp', split_axis=0, concat_axis=0, tiled=True)  6.32 us
  transfers between devices with their start and end apart: 5, of which 3 were waited for; matrix products, arithmetic and copies ran while one was open for 20% of the time, Pallas kernels for 0%

commit v1 on v0

--- a/solution.py
+++ b/solution.py
@@ -3,6 +3,8 @@
 import jax
 import jax.numpy as jnp
 from jax import lax
+from jax.experimental import pallas as pl
+from jax.experimental.pallas import tpu as pltpu
 from jax.sharding import PartitionSpec as P
 
 MODEL_WIDTH = 8192
@@ -153,7 +155,492 @@
     )
 
 
+N = 4
+RANK = 64
+HALF = 128
+CHUNK = 64
+ROWS_STEP = 416
+COL_STEP = 256
+NT = (((1,), (1,)), ((), ()))
+NN = (((1,), (0,)), ((), ()))
+TN = (((0,), (0,)), ((), ()))
+
+
+def fused_kernel(
+    owners_ref,
+    position_ref,
+    x_ref,
+    v_ref,
+    dw_ref,
+    uw_ref,
+    dm_ref,
+    ds_ref,
+    um_ref,
+    us_ref,
+    g_ref,
+    values_ref,
+    ndw_ref,
+    nuw_ref,
+    ndm_ref,
+    nds_ref,
+    num_ref,
+    nus_ref,
+    line,
+    uall,
+    other,
+    psend,
+    prec,
+    own_base,
+    bpart,
+    lpart,
+    back_half,
+    low_half,
+    acc,
+    csend,
+    crecv,
+    esend,
+    erecv,
+    extra,
+    send_a,
+    recv_a,
+    send_z,
+    recv_z,
+    send_y,
+    recv_y,
+    send_p,
+    recv_p,
+    send_b,
+    recv_b,
+    send_l,
+    recv_l,
+    send_c,
+    recv_c,
+    send_e,
+    recv_e,
+):
+    grp = lax.axis_index("groups")
+    z = lax.axis_index("fsdp")
+    own = lax.axis_index("owner")
+    tokens = x_ref.shape[0]
+    blocks = tokens // BLOCK
+    width = x_ref.shape[1]
+    down_factor = 1.0 / math.sqrt(MODEL_WIDTH)
+    up_factor = branch_scale / math.sqrt(RANK)
+    bf = jnp.bfloat16
+    f32 = jnp.float32
+
+    def remote(src, dst, ssem, rsem, **where):
+        return pltpu.make_async_remote_copy(
+            src_ref=src,
+            dst_ref=dst,
+            send_sem=ssem,
+            recv_sem=rsem,
+            device_id=where,
+            device_id_type=pl.DeviceIdType.MESH,
+        )
+
+    def mod(i):
+        return lax.rem(i + N, N)
+
+    uall[z] = uw_ref[0].astype(bf)
+    line[z, 0] = dw_ref[0].astype(bf)
+    for c in range(2):
+        first = pl.multiple_of(grp * HALF + c * CHUNK, CHUNK)
+        line[z, 1 + c] = v_ref[pl.ds(first, CHUNK), :]
+        first = pl.multiple_of((1 - grp) * HALF + c * CHUNK, CHUNK)
+        other[z, c] = v_ref[pl.ds(first, CHUNK), :]
+
+    barrier = pltpu.get_barrier_semaphore()
+    for k in range(1, N):
+        pl.semaphore_signal(
+            barrier, inc=1, device_id={"fsdp": mod(z + k)}, device_id_type=pl.DeviceIdType.MESH
+        )
+        pl.semaphore_signal(
+            barrier, inc=1, device_id={"owner": mod(own + k)}, device_id_type=pl.DeviceIdType.MESH
+        )
+    pl.semaphore_signal(
+        barrier, inc=1, device_id={"groups": 1 - grp}, device_id_type=pl.DeviceIdType.MESH
+    )
+    pl.semaphore_wait(barrier, 7)
+
+    def copy_a(k):
+        return remote(
+            uall.at[z], uall.at[z], send_a.at[k - 1], recv_a.at[k - 1], fsdp=mod(z + k)
+        )
+
+    def copy_z(s, kind, way):
+        return remote(
+            line.at[s, kind],
+            line.at[s, kind],
+            send_z.at[s, kind, way],
+            recv_z.at[s, kind],
+            fsdp=mod(z - 1 + 2 * way),
+        )
+
+    def copy_y(s, c):
+        return remote(
+            line.at[s, 1 + c],
+            other.at[s, c],
+            send_y.at[s, c],
+            recv_y.at[s, c],
+            groups=1 - grp,
+        )
+
+    def copy_p(s, h):
+        k = mod(s - own)
+        return remote(
+            psend.at[s, h], prec.at[h, k - 1], send_p.at[s, h], recv_p.at[h, k - 1], owner=s
+        )
+
+    def copy_b(k):
+        return remote(
+            bpart.at[0], bpart.at[k], send_b.at[k - 1], recv_b.at[k - 1], owner=mod(own + k)
+        )
+
+    def copy_l(k):
+        return remote(
+            lpart.at[0], lpart.at[k], send_l.at[k - 1], recv_l.at[k - 1], owner=mod(own + k)
+        )
+
+    def copy_c(k):
+        to = mod(z + k)
+        return remote(
+            csend.at[to], crecv.at[k - 1], send_c.at[k - 1], recv_c.at[k - 1], fsdp=to
+        )
+
+    def copy_e(k):
+        to = mod(z + k)
+        return remote(
+            esend.at[to], erecv.at[k - 1], send_e.at[k - 1], recv_e.at[k - 1], fsdp=to
+        )
+
+    for k in range(1, N):
+        copy_a(k).start()
+    for kind in range(3):
+        for way in range(2):
+
+            @pl.when((z > 0) if way == 0 else (z < N - 1))
+            def _():
+                copy_z(z, kind, way).start()
+
+    def product(s, mine):
+        h = grp if mine else 1 - grp
+        if mine:
+            rows = line[s, 1:3].reshape(HALF, width)
+        else:
+            rows = other[s].reshape(HALF, width)
+
+        @pl.loop(0, tokens // ROWS_STEP)
+        def _(i):
+            at = pl.ds(pl.multiple_of(i * ROWS_STEP, ROWS_STEP), ROWS_STEP)
+            part = lax.dot_general(x_ref[at, :], rows, NT, preferred_element_type=f32)
+
+            @pl.when(s == own)
+            def _():
+                own_base[h, at, :] = part
+
+            @pl.when(s != own)
+            def _():
+                psend[s, h, at, :] = part.astype(bf)
+
+        @pl.when(s != own)
+        def _():
+            copy_p(s, h).start()
+
+    def sources(d):
+        return ((z + d, z + d < N, 0), (z - d, z - d >= 0, 1))
+
+    def forward(d):
+        for kind in range(3):
+            for s, valid, way in sources(d):
+
+                @pl.when(valid)
+                def _():
+                    copy_z(s, kind, way).wait_recv()
+                    if d < N - 1:
+
+                        @pl.when((z > 0) if way == 0 else (z < N - 1))
+                        def _():
+                            copy_z(s, kind, way).start()
+
+                    if kind > 0:
+                        copy_y(s, kind - 1).start()
+
+    def line_products(d):
+        for s, valid, way in sources(d):
+
+            @pl.when(valid)
+            def _():
+                product(s, True)
+
+    def cross_products(d):
+        for s, valid, way in sources(d):
+
+            @pl.when(valid)
+            def _():
+                copy_y(s, 0).wait_recv()
+                copy_y(s, 1).wait_recv()
+                product(s, False)
+
+    def block_rows(b):
+        return pl.ds(pl.multiple_of(b * BLOCK, BLOCK), BLOCK)
+
+    product(z, True)
+
+    for k in range(1, N):
+        copy_a(k).wait_recv()
+
+    @pl.loop(0, blocks)
+    def _(b):
+        part = lax.dot_general(
+            uall[owners_ref[b]], g_ref[block_rows(b), :], NT, preferred_element_type=f32
+        )
+        bpart[0, b] = (part * up_factor).astype(bf)
+
+    for k in range(1, N):
+        copy_b(k).start()
+    product(z, False)
+    for k in range(1, N):
+        copy_b(k).wait_recv()
+
+    @pl.loop(0, blocks)
+    def _(b):
+        total = (bpart[0, b].astype(f32) + bpart[1, b].astype(f32)) + (
+            bpart[2, b].astype(f32) + bpart[3, b].astype(f32)
+        )
+        back_half[b] = total.astype(bf)
+
+    @pl.loop(0, width // COL_STEP)
+    def _(i):
+        at = pl.ds(pl.multiple_of(i * COL_STEP, COL_STEP), COL_STEP)
+        for p in range(N):
+            total = None
+            for b in range(p, blocks, N):
+                part = lax.dot_general(
+                    back_half[b],
+                    x_ref[b * BLOCK : (b + 1) * BLOCK, at],
+                    NN,
+                    preferred_element_type=f32,
+                )
+                total = part if total is None else total + part
+            acc[p, :, at] = (total * down_factor).astype(bf)
+
+    for f in range(N):
+        csend[f] = acc[position_ref[f]]
+
+    forward(1)
+    line_products(1)
+    forward(2)
+    line_products(2)
+    cross_products(1)
+    forward(3)
+    for k in range(1, N):
+        copy_c(k).start()
+
+    @pl.loop(0, blocks)
+    def _(b):
+        part = lax.dot_general(
+            line[owners_ref[b], 0], x_ref[block_rows(b), :], NT, preferred_element_type=f32
+        )
+        lpart[0, b] = (part * down_factor).astype(bf)
+
+    for k in range(1, N):
+        copy_l(k).start()
+    line_products(3)
+    cross_products(2)
+    for k in range(1, N):
+        copy_l(k).wait_recv()
+
+    @pl.loop(0, blocks)
+    def _(b):
+        total = (lpart[0, b].astype(f32) + lpart[1, b].astype(f32)) + (
+            lpart[2, b].astype(f32) + lpart[3, b].astype(f32)
+        )
+        half = total.astype(bf)
+        low_half[b] = half
+        extra[block_rows(b), :] = up_factor * lax.dot_general(
+            half, uall[owners_ref[b]], TN, preferred_element_type=f32
+        )
+
+    for p in range(N):
+        total = None
+        for b in range(p, blocks, N):
+            part = lax.dot_general(
+                low_half[b],
+                g_ref[b * BLOCK : (b + 1) * BLOCK, :],
+                NN,
+                preferred_element_type=f32,
+            )
+            total = part if total is None else total + part
+        acc[p, :, 0:256] = (total * up_factor).astype(bf)
+    for f in range(N):
+        esend[f] = acc[position_ref[f], :, 0:256]
+    for k in range(1, N):
+        copy_e(k).start()
+    cross_products(3)
+
+    for k in range(1, N):
+        copy_e(k).wait_recv()
+    gradient = (esend[z].astype(f32) + erecv[0].astype(f32)) + (
+        erecv[1].astype(f32) + erecv[2].astype(f32)
+    )
+    nuw_ref[0], num_ref[0], nus_ref[0] = adam_weight_update(
+        uw_ref[0], um_ref[0], us_ref[0], gradient
+    )
+    for k in range(1, N):
+        copy_c(k).wait_recv()
+
+    @pl.loop(0, width // COL_STEP)
+    def _(i):
+        at = pl.ds(pl.multiple_of(i * COL_STEP, COL_STEP), COL_STEP)
+        total = (csend[z, :, at].astype(f32) + crecv[0, :, at].astype(f32)) + (
+            crecv[1, :, at].astype(f32) + crecv[2, :, at].astype(f32)
+        )
+        ndw_ref[0, :, at], ndm_ref[0, :, at], nds_ref[0, :, at] = adam_weight_update(
+            dw_ref[0, :, at], dm_ref[0, :, at], ds_ref[0, :, at], total
+        )
+
+    for h in range(2):
+        for k in range(1, N):
+            remote(
+                psend.at[0, h], prec.at[h, k - 1], send_p.at[0, h], recv_p.at[h, k - 1], owner=mod(own + k)
+            ).wait_recv()
+        cols = slice(h * HALF, (h + 1) * HALF)
+
+        @pl.loop(0, tokens // ROWS_STEP)
+        def _(i):
+            at = pl.ds(pl.multiple_of(i * ROWS_STEP, ROWS_STEP), ROWS_STEP)
+            total = (own_base[h, at, :] + prec[h, 0, at, :].astype(f32)) + (
+                prec[h, 1, at, :].astype(f32) + prec[h, 2, at, :].astype(f32)
+            )
+            values_ref[at, cols] = (total + extra[at, cols]).astype(bf)
+
+    for k in range(1, N):
+        copy_a(k).wait_send()
+        copy_b(k).wait_send()
+        copy_l(k).wait_send()
+        copy_c(k).wait_send()
+        copy_e(k).wait_send()
+    for kind in range(3):
+        for way in range(2):
+            room = (z > 0) if way == 0 else (z < N - 1)
+
+            @pl.when(room)
+            def _():
+                copy_z(z, kind, way).wait_send()
+
+            for d in range(1, N - 1):
+                s, valid, _ = sources(d)[way]
+
+                @pl.when(valid & room)
+                def _():
+                    copy_z(s, kind, way).wait_send()
+
+    for k in range(1, N):
+        for c in range(2):
+            copy_y(mod(z + k), c).wait_send()
+            copy_p(mod(own + k), c).wait_send()
+
+
+def per_device_fused(
+    inputs,
+    value_matrix,
+    adapter_down_weight,
+    adapter_up_weight,
+    down_first_moment,
+    down_second_moment,
+    up_first_moment,
+    up_second_moment,
+    output_gradient,
+    tenant_of_block,
+    tenant_storage_slot,
+):
+    my_index = lax.axis_index("fsdp")
+    tokens, width = inputs.shape
+    blocks = tokens // BLOCK
+    tenants = lax.dynamic_slice_in_dim(tenant_of_block, my_index * blocks, blocks)
+    ids = jnp.arange(N, dtype=jnp.int32)
+    owners = jnp.sum(
+        jnp.where(tenants[:, None] == ids[None, :], tenant_storage_slot[None, :], 0), axis=1
+    )
+    position = jnp.sum(
+        jnp.where(owners[None, :N] == ids[:, None], ids[None, :], 0), axis=1
+    )
+    bf, f32 = jnp.bfloat16, jnp.float32
+    big = jax.ShapeDtypeStruct((1, RANK, width), f32)
+    small = jax.ShapeDtypeStruct((1, RANK, 256), f32)
+    dma = pltpu.SemaphoreType.DMA
+    vmem = pl.BlockSpec(memory_space=pltpu.VMEM)
+    smem = pl.BlockSpec(memory_space=pltpu.SMEM)
+    values, ndw, nuw, ndm, nds, num, nus = pl.pallas_call(
+        fused_kernel,
+        out_shape=(
+            jax.ShapeDtypeStruct((tokens, 256), bf),
+            big,
+            small,
+            big,
+            big,
+            small,
+            small,
+        ),
+        in_specs=[smem] * 2 + [vmem] * 9,
+        out_specs=[vmem] * 7,
+        scratch_shapes=[
+            pltpu.VMEM((N, 3, CHUNK, width), bf),
+            pltpu.VMEM((N, RANK, 256), bf),
+            pltpu.VMEM((N, 2, CHUNK, width), bf),
+            pltpu.VMEM((N, 2, tokens, HALF), bf),
+            pltpu.VMEM((2, 3, tokens, HALF), bf),
+            pltpu.VMEM((2, tokens, HALF), f32),
+            pltpu.VMEM((N, blocks, RANK, BLOCK), bf),
+            pltpu.VMEM((N, blocks, RANK, BLOCK), bf),
+            pltpu.VMEM((blocks, RANK, BLOCK), bf),
+            pltpu.VMEM((blocks, RANK, BLOCK), bf),
+            pltpu.VMEM((N, RANK, width), bf),
+            pltpu.VMEM((N, RANK, width), bf),
+            pltpu.VMEM((N - 1, RANK, width), bf),
+            pltpu.VMEM((N, RANK, 256), bf),
+            pltpu.VMEM((N - 1, RANK, 256), bf),
+            pltpu.VMEM((tokens, 256), f32),
+            dma((3,)),
+            dma((3,)),
+            dma((N, 3, 2)),
+            dma((N, 3)),
+            dma((N, 2)),
+            dma((N, 2)),
+            dma((N, 2)),
+            dma((2, 3)),
+            dma((3,)),
+            dma((3,)),
+            dma((3,)),
+            dma((3,)),
+            dma((3,)),
+            dma((3,)),
+            dma((3,)),
+            dma((3,)),
+        ],
+        compiler_params=pltpu.CompilerParams(
+            collective_id=0, has_side_effects=True, vmem_limit_bytes=56 * 1024 * 1024
+        ),
+    )(
+        owners,
+        position,
+        inputs,
+        value_matrix,
+        adapter_down_weight,
+        adapter_up_weight,
+        down_first_moment,
+        down_second_moment,
+        up_first_moment,
+        up_second_moment,
+        output_gradient,
+    )
+    return values, ndw, nuw, ndm, nds, num, nus
+
+
 def solution(mesh):
+    sizes = mesh.shape
+    fused = sizes["groups"] == 2 and sizes["fsdp"] == N and sizes["owner"] == N
     in_specs = (
         P(("groups", "fsdp"), "owner"),
         P("fsdp", "owner"),
@@ -177,5 +664,5 @@
         P(("groups", "fsdp"), None, "owner"),
     )
     return jax.shard_map(
-        per_device, mesh=mesh, in_specs=in_specs, out_specs=out_specs, check_vma=False
-    )
+        per_device_fused if fused else per_device, mesh=mesh, in_specs=in_specs, out_specs=out_specs, check_vma=False
+    )

time: 225 us -> 128 us (0.57)
  the two profiles are of different devices: /device:TPU:0 before, /device:TPU:7 now
where the time goes in v1:
time: 128 us; the launch traced here: 127 us
  Pallas kernels  112 us (88%)
  local copies, waits for them, and re-layouts  12.9 us (10%)
  other arithmetic  1.37 us (1%)
    pallas_call x1, Pallas kernels, per_device_fused(): pl.pallas_call(fused_kernel, out_shape=(jax.ShapeDtypeStruct((tokens, 256...  112 us
    unnamed x9, local copies, waits for them, and re-layouts  12.1 us

profile of v1, /device:TPU:7, one launch (start us, length us, event | category | flops | bytes accessed | tf_op | source)
XLA Modules:
  0.0 127.1 jit_solution(5831868437821221687)
XLA Ops:
  0.6 0.7 dynamic_slice.3
  1.4 0.7 select_reduce_fusion.1.owners_ref
  2.1 0.0 copy-start
  2.1 0.6 select_reduce_fusion.position_ref
  2.7 0.0 copy-done
  2.7 112.2 %shard_map.162 = (bf16[1664,256]{1,0:T(8,128)(2,1)}, f32[1,64,2048]{2,1,0:T(8,128)}, f32[1,64,256]{2,1,0:T(8,128)}, f32[1,64,2048]{2,1,0:T(8,128)}, f32[1,64,204...) custom-call(s32[13]{0:T(128)} %copy-done, s32[4]{0:T(128)} %select_reduce_fusion.position_ref, ...), custom_call_target="tpu_custom_call" | custom-call | tf_op jit(solution)/shard_map/pallas_call | solution.py:575
  115.0 2.1 %copy.25 = bf16[1664,256]{1,0:T(8,128)(2,1)} copy(bf16[1664,256]{1,0:T(8,128)(2,1)} %get-tuple-element.14) | data formatting | bytes 1703936
  117.1 1.9 %copy.26 = f32[1,64,2048]{2,1,0:T(8,128)} copy(f32[1,64,2048]{2,1,0:T(8,128)} %get-tuple-element.15) | data formatting | bytes 1048576
  118.9 1.5 %copy.27 = f32[1,64,256]{2,1,0:T(8,128)} copy(f32[1,64,256]{2,1,0:T(8,128)} %get-tuple-element.16) | data formatting | bytes 131072
  120.4 1.9 %copy.28 = f32[1,64,2048]{2,1,0:T(8,128)} copy(f32[1,64,2048]{2,1,0:T(8,128)} %get-tuple-element.17) | data formatting | bytes 1048576
  122.3 1.9 %copy.29 = f32[1,64,2048]{2,1,0:T(8,128)} copy(f32[1,64,2048]{2,1,0:T(8,128)} %get-tuple-element.18) | data formatting | bytes 1048576
  124.2 1.5 %copy.30 = f32[1,64,256]{2,1,0:T(8,128)} copy(f32[1,64,256]{2,1,0:T(8,128)} %get-tuple-element.19) | data formatting | bytes 131072
  125.6 1.5 %copy.31 = f32[1,64,256]{2,1,0:T(8,128)} copy(f32[1,64,256]{2,1,0:T(8,128)} %get-tuple-element.20) | data formatting | bytes 131072
Async XLA Ops:
  2.1 0.6 copy-start

commit v2 on v1

--- a/solution.py
+++ b/solution.py
@@ -167,24 +167,19 @@
 
 
 def fused_kernel(
-    owners_ref,
-    position_ref,
-    x_ref,
+    tenant_ref,
+    storage_ref,
+    x_hbm,
     v_ref,
     dw_ref,
     uw_ref,
-    dm_ref,
-    ds_ref,
-    um_ref,
-    us_ref,
+    g_hbm,
+    values_ref,
+    grad_down_ref,
+    grad_up_ref,
+    x_ref,
     g_ref,
-    values_ref,
-    ndw_ref,
-    nuw_ref,
-    ndm_ref,
-    nds_ref,
-    num_ref,
-    nus_ref,
+    dall,
     line,
     uall,
     other,
@@ -217,6 +212,7 @@
     recv_c,
     send_e,
     recv_e,
+    load_sem,
 ):
     grp = lax.axis_index("groups")
     z = lax.axis_index("fsdp")
@@ -229,6 +225,20 @@
     bf = jnp.bfloat16
     f32 = jnp.float32
 
+    load_g = pltpu.make_async_copy(g_hbm, g_ref, load_sem.at[0])
+    load_x = pltpu.make_async_copy(x_hbm, x_ref, load_sem.at[1])
+    load_g.start()
+    load_x.start()
+
+    def owner_of(b):
+        return storage_ref[tenant_ref[z * blocks + b]]
+
+    def position_of(f):
+        place = 0
+        for p in range(1, N):
+            place = jnp.where(owner_of(p) == f, p, place)
+        return place
+
     def remote(src, dst, ssem, rsem, **where):
         return pltpu.make_async_remote_copy(
             src_ref=src,
@@ -243,10 +253,10 @@
         return lax.rem(i + N, N)
 
     uall[z] = uw_ref[0].astype(bf)
-    line[z, 0] = dw_ref[0].astype(bf)
+    dall[z] = dw_ref[0].astype(bf)
     for c in range(2):
         first = pl.multiple_of(grp * HALF + c * CHUNK, CHUNK)
-        line[z, 1 + c] = v_ref[pl.ds(first, CHUNK), :]
+        line[z, c] = v_ref[pl.ds(first, CHUNK), :]
         first = pl.multiple_of((1 - grp) * HALF + c * CHUNK, CHUNK)
         other[z, c] = v_ref[pl.ds(first, CHUNK), :]
 
@@ -269,9 +279,10 @@
         )
 
     def copy_z(s, kind, way):
-        return remote(
-            line.at[s, kind],
-            line.at[s, kind],
+        piece = dall.at[s] if kind == 0 else line.at[s, kind - 1]
+        return remote(
+            piece,
+            piece,
             send_z.at[s, kind, way],
             recv_z.at[s, kind],
             fsdp=mod(z - 1 + 2 * way),
@@ -279,7 +290,7 @@
 
     def copy_y(s, c):
         return remote(
-            line.at[s, 1 + c],
+            line.at[s, c],
             other.at[s, c],
             send_y.at[s, c],
             recv_y.at[s, c],
@@ -316,17 +327,21 @@
 
     for k in range(1, N):
         copy_a(k).start()
-    for kind in range(3):
+
+    def send_own(kind):
         for way in range(2):
 
             @pl.when((z > 0) if way == 0 else (z < N - 1))
             def _():
                 copy_z(z, kind, way).start()
+
+    send_own(0)
+    send_own(1)
 
     def product(s, mine):
         h = grp if mine else 1 - grp
         if mine:
-            rows = line[s, 1:3].reshape(HALF, width)
+            rows = line[s].reshape(HALF, width)
         else:
             rows = other[s].reshape(HALF, width)
 
@@ -350,21 +365,27 @@
     def sources(d):
         return ((z + d, z + d < N, 0), (z - d, z - d >= 0, 1))
 
-    def forward(d):
-        for kind in range(3):
-            for s, valid, way in sources(d):
-
-                @pl.when(valid)
-                def _():
-                    copy_z(s, kind, way).wait_recv()
-                    if d < N - 1:
-
-                        @pl.when((z > 0) if way == 0 else (z < N - 1))
-                        def _():
-                            copy_z(s, kind, way).start()
-
-                    if kind > 0:
-                        copy_y(s, kind - 1).start()
+    def forward(d, kind):
+        for s, valid, way in sources(d):
+
+            @pl.when(valid)
+            def _():
+                copy_z(s, kind, way).wait_recv()
+                if d < N - 1:
+
+                    @pl.when((z > 0) if way == 0 else (z < N - 1))
+                    def _():
+                        copy_z(s, kind, way).start()
+
+                if kind > 0:
+                    copy_y(s, kind - 1).start()
+
+    def sent_forward(d, kind):
+        for s, valid, way in sources(d):
+
+            @pl.when(valid & ((z > 0) if way == 0 else (z < N - 1)))
+            def _():
+                copy_z(s, kind, way).wait_send()
 
     def line_products(d):
         for s, valid, way in sources(d):
@@ -385,20 +406,23 @@
     def block_rows(b):
         return pl.ds(pl.multiple_of(b * BLOCK, BLOCK), BLOCK)
 
-    product(z, True)
-
+    load_g.wait()
     for k in range(1, N):
         copy_a(k).wait_recv()
 
     @pl.loop(0, blocks)
     def _(b):
         part = lax.dot_general(
-            uall[owners_ref[b]], g_ref[block_rows(b), :], NT, preferred_element_type=f32
+            uall[owner_of(b)], g_ref[block_rows(b), :], NT, preferred_element_type=f32
         )
         bpart[0, b] = (part * up_factor).astype(bf)
 
     for k in range(1, N):
         copy_b(k).start()
+    load_x.wait()
+    product(z, True)
+    forward(1, 0)
+    send_own(2)
     product(z, False)
     for k in range(1, N):
         copy_b(k).wait_recv()
@@ -426,28 +450,26 @@
             acc[p, :, at] = (total * down_factor).astype(bf)
 
     for f in range(N):
-        csend[f] = acc[position_ref[f]]
-
-    forward(1)
+        csend[f] = acc[position_of(f)]
+
+    forward(2, 0)
+    forward(1, 1)
+    forward(1, 2)
     line_products(1)
-    forward(2)
-    line_products(2)
-    cross_products(1)
-    forward(3)
-    for k in range(1, N):
-        copy_c(k).start()
-
+    forward(3, 0)
+    forward(2, 1)
     @pl.loop(0, blocks)
     def _(b):
         part = lax.dot_general(
-            line[owners_ref[b], 0], x_ref[block_rows(b), :], NT, preferred_element_type=f32
+            dall[owner_of(b)], x_ref[block_rows(b), :], NT, preferred_element_type=f32
         )
         lpart[0, b] = (part * down_factor).astype(bf)
 
     for k in range(1, N):
         copy_l(k).start()
-    line_products(3)
-    cross_products(2)
+    forward(2, 2)
+    line_products(2)
+    cross_products(1)
     for k in range(1, N):
         copy_l(k).wait_recv()
 
@@ -459,7 +481,7 @@
         half = total.astype(bf)
         low_half[b] = half
         extra[block_rows(b), :] = up_factor * lax.dot_general(
-            half, uall[owners_ref[b]], TN, preferred_element_type=f32
+            half, uall[owner_of(b)], TN, preferred_element_type=f32
         )
 
     for p in range(N):
@@ -474,18 +496,23 @@
             total = part if total is None else total + part
         acc[p, :, 0:256] = (total * up_factor).astype(bf)
     for f in range(N):
-        esend[f] = acc[position_ref[f], :, 0:256]
+        esend[f] = acc[position_of(f), :, 0:256]
     for k in range(1, N):
         copy_e(k).start()
+    forward(3, 1)
+    forward(3, 2)
+    for kind in (1, 2):
+        sent_forward(2, kind)
+    for k in range(1, N):
+        copy_c(k).start()
+    line_products(3)
+    cross_products(2)
     cross_products(3)
 
     for k in range(1, N):
         copy_e(k).wait_recv()
-    gradient = (esend[z].astype(f32) + erecv[0].astype(f32)) + (
+    grad_up_ref[0] = (esend[z].astype(f32) + erecv[0].astype(f32)) + (
         erecv[1].astype(f32) + erecv[2].astype(f32)
-    )
-    nuw_ref[0], num_ref[0], nus_ref[0] = adam_weight_update(
-        uw_ref[0], um_ref[0], us_ref[0], gradient
     )
     for k in range(1, N):
         copy_c(k).wait_recv()
@@ -493,11 +520,8 @@
     @pl.loop(0, width // COL_STEP)
     def _(i):
         at = pl.ds(pl.multiple_of(i * COL_STEP, COL_STEP), COL_STEP)
-        total = (csend[z, :, at].astype(f32) + crecv[0, :, at].astype(f32)) + (
+        grad_down_ref[0, :, at] = (csend[z, :, at].astype(f32) + crecv[0, :, at].astype(f32)) + (
             crecv[1, :, at].astype(f32) + crecv[2, :, at].astype(f32)
-        )
-        ndw_ref[0, :, at], ndm_ref[0, :, at], nds_ref[0, :, at] = adam_weight_update(
-            dw_ref[0, :, at], dm_ref[0, :, at], ds_ref[0, :, at], total
         )
 
     for h in range(2):
@@ -513,7 +537,7 @@
             total = (own_base[h, at, :] + prec[h, 0, at, :].astype(f32)) + (
                 prec[h, 1, at, :].astype(f32) + prec[h, 2, at, :].astype(f32)
             )
-            values_ref[at, cols] = (total + extra[at, cols]).astype(bf)
+            values_ref[at, cols] = total + extra[at, cols]
 
     for k in range(1, N):
         copy_a(k).wait_send()
@@ -529,12 +553,8 @@
             def _():
                 copy_z(z, kind, way).wait_send()
 
-            for d in range(1, N - 1):
-                s, valid, _ = sources(d)[way]
-
-                @pl.when(valid & room)
-                def _():
-                    copy_z(s, kind, way).wait_send()
+        sent_forward(1, kind)
+    sent_forward(2, 0)
 
     for k in range(1, N):
         for c in range(2):
@@ -555,38 +575,29 @@
     tenant_of_block,
     tenant_storage_slot,
 ):
-    my_index = lax.axis_index("fsdp")
     tokens, width = inputs.shape
     blocks = tokens // BLOCK
-    tenants = lax.dynamic_slice_in_dim(tenant_of_block, my_index * blocks, blocks)
-    ids = jnp.arange(N, dtype=jnp.int32)
-    owners = jnp.sum(
-        jnp.where(tenants[:, None] == ids[None, :], tenant_storage_slot[None, :], 0), axis=1
-    )
-    position = jnp.sum(
-        jnp.where(owners[None, :N] == ids[:, None], ids[None, :], 0), axis=1
-    )
     bf, f32 = jnp.bfloat16, jnp.float32
     big = jax.ShapeDtypeStruct((1, RANK, width), f32)
     small = jax.ShapeDtypeStruct((1, RANK, 256), f32)
     dma = pltpu.SemaphoreType.DMA
     vmem = pl.BlockSpec(memory_space=pltpu.VMEM)
     smem = pl.BlockSpec(memory_space=pltpu.SMEM)
-    values, ndw, nuw, ndm, nds, num, nus = pl.pallas_call(
+    hbm = pl.BlockSpec(memory_space=pl.ANY)
+    values, grad_down, grad_up = pl.pallas_call(
         fused_kernel,
         out_shape=(
-            jax.ShapeDtypeStruct((tokens, 256), bf),
+            jax.ShapeDtypeStruct((tokens, 256), f32),
             big,
             small,
-            big,
-            big,
-            small,
-            small,
         ),
-        in_specs=[smem] * 2 + [vmem] * 9,
-        out_specs=[vmem] * 7,
+        in_specs=[smem, smem, hbm, vmem, vmem, vmem, hbm],
+        out_specs=[vmem] * 3,
         scratch_shapes=[
-            pltpu.VMEM((N, 3, CHUNK, width), bf),
+            pltpu.VMEM((tokens, width), bf),
+            pltpu.VMEM((tokens, 256), bf),
+            pltpu.VMEM((N, RANK, width), bf),
+            pltpu.VMEM((N, 2, CHUNK, width), bf),
             pltpu.VMEM((N, RANK, 256), bf),
             pltpu.VMEM((N, 2, CHUNK, width), bf),
             pltpu.VMEM((N, 2, tokens, HALF), bf),
@@ -618,24 +629,27 @@
             dma((3,)),
             dma((3,)),
             dma((3,)),
+            dma((2,)),
         ],
         compiler_params=pltpu.CompilerParams(
             collective_id=0, has_side_effects=True, vmem_limit_bytes=56 * 1024 * 1024
         ),
     )(
-        owners,
-        position,
+        tenant_of_block,
+        tenant_storage_slot,
         inputs,
         value_matrix,
         adapter_down_weight,
         adapter_up_weight,
-        down_first_moment,
-        down_second_moment,
-        up_first_moment,
-        up_second_moment,
         output_gradient,
     )
-    return values, ndw, nuw, ndm, nds, num, nus
+    ndw, ndm, nds = adam_weight_update(
+        adapter_down_weight, down_first_moment, down_second_moment, grad_down
+    )
+    nuw, num, nus = adam_weight_update(
+        adapter_up_weight, up_first_moment, up_second_moment, grad_up
+    )
+    return values.astype(bf), ndw, nuw, ndm, nds, num, nus
 
 
 def solution(mesh):

time: 128 us -> 103 us (0.80)
  Pallas kernels: 112 us -> 95.1 us
  local copies, waits for them, and re-layouts: 12.9 us -> 0.03 us
  other arithmetic: 1.37 us -> 6.41 us
    pallas_call x1, Pallas kernels: 112 us -> 95.1 us  [per_device_fused(): pl.pallas_call(fused_kernel, out_shape=(jax.ShapeDtypeStruct((tokens, 256...]
    unnamed x9 -> x12, local copies, waits for them, and re-layouts: 12.1 us -> 0.03 us
    sub x0 -> x2, other arithmetic: none -> 3.97 us  [adam_weight_update(): new_weights = weights - learning_rate * (direction + decay_rate * weights)]
    convert_element_type x0 -> x1, other arithmetic: none -> 2.44 us  [per_device_fused(): return (values.astype(bf), ndw, nuw, ndm, nds, num, nus)]
    reduce_sum x2 -> x0, other arithmetic: 1.37 us -> none  [the longest x1 0.74 us: per_device_fused(): jnp.sum(jnp.where(tenants[:, None] == ids[None, :], tenant_storage_slot[N...]
where the time goes in v2:
time: 103 us; the launch traced here: 102 us
  Pallas kernels  95.1 us (92%)
  other arithmetic  6.41 us (6%)
    pallas_call x1, Pallas kernels, per_device_fused(): pl.pallas_call(fused_kernel, out_shape=(jax.ShapeDtypeStruct((tokens, 256...  95.1 us
    sub x2, other arithmetic, adam_weight_update(): new_weights = weights - learning_rate * (direction + decay_rate * weights)  3.97 us
    convert_element_type x1, other arithmetic, per_device_fused(): return (values.astype(bf), ndw, nuw, ndm, nds, num, nus)  2.44 us

profile of v2, /device:TPU:7, one launch (start us, length us, event | category | flops | bytes accessed | tf_op | source)
XLA Modules:
  0.0 102.3 jit_solution(17630154086838963735)
XLA Ops:
  0.6 0.0 copy-start.3
  0.6 0.0 copy-start
  0.7 0.0 copy-start.5
  0.7 0.0 copy-start.4
  0.7 0.0 copy-start.2
  0.7 0.0 copy-start.1
  0.7 95.1 %shard_map.162 = (f32[1664,256]{1,0:T(8,128)}, f32[1,64,2048]{2,1,0:T(8,128)}, f32[1,64,256]{2,1,0:T(8,128)}) custom-call(s32[52]{0:T(128)} %tenant_ref.1, s32[4]{0:T(128)} %storage_ref.1, bf16[1664,2048]{1,0:T(8,128)(2,1)} %x_hbm.1, bf16[256,2048]{1,0:T(8,128)(2,1)} %v_ref.1, f32[1,64,2048]{2,1,0:T(8,128)} %dw_ref.1, f32[1,64,256]{2,1,0:T(8,128)} %uw_ref.1, ...), custom_call_target="tpu_custom_call" | custom-call | tf_op jit(solution)/shard_map/pallas_call | solution.py:587
  95.8 2.4 %convert_element_type.3 = bf16[1664,256]{1,0:T(8,128)(2,1)} convert(f32[1664,256]{1,0:T(8,128)} %get-tuple-element.10) | non-fusion elementwise | flops 425984 | bytes 2555904 | tf_op jit(solution)/shard_map/convert_element_type | solution.py:652
  98.3 0.0 copy-done.3
  98.3 0.0 copy-done.5
  98.3 0.0 copy-done.4
  98.3 1.5 %multiply_subtract_fusion.1 = (f32[1,64,256]{2,1,0:T(8,128)}, f32[1,64,256]{2,1,0:T(8,128)}, f32[1,64,256]{2,1,0:T(8,128)}) fusion(f32[1,64,256]{2,1,0:T(8,128)S(1)} %copy-done.3, f32[1,64,256]{2,1,0:T(8,128)} %get-tuple-element.12, f32[1,64,256]{2,1,0:T(8,128)S(1)} %copy-done.4, f32[1,64,256]{2,1,0:T(8,128)S(1)} %copy-done.5), kind=kLoop, calls=%fused_computation.6 | loop fusion | flops 245760 | bytes 458752 | tf_op jit(solution)/shard_map/sub | solution.py:28
  99.8 0.0 copy-done
  99.8 0.0 copy-done.2
  99.8 0.0 copy-done.1
  99.8 2.4 %multiply_subtract_fusion = (f32[1,64,2048]{2,1,0:T(8,128)}, f32[1,64,2048]{2,1,0:T(8,128)}, f32[1,64,2048]{2,1,0:T(8,128)}) fusion(f32[1,64,2048]{2,1,0:T(8,128)S(1)} %copy-done, f32[1,64,2048]{2,1,0:T(8,128)} %get-tuple-element.11, f32[1,64,2048]{2,1,0:T(8,128)S(1)} %copy-done.1, f32[1,64,2048]{2,1,0:T(8,128)S(1)} %copy-done.2), kind=kLoop, calls=%fused_computation.2 | loop fusion | flops 1966080 | bytes 3670016 | tf_op jit(solution)/shard_map/sub | solution.py:28
Async XLA Ops:
  0.6 97.6 %copy-start.3 = (f32[1,64,256]{2,1,0:T(8,128)S(1)}, f32[1,64,256]{2,1,0:T(8,128)}, u32[]{:S(2)}) copy-start(f32[1,64,256]{2,1,0:T(8,128)} %uw_ref.1) | copy-start | bytes 196612
  0.6 99.2 %copy-start = (f32[1,64,2048]{2,1,0:T(8,128)S(1)}, f32[1,64,2048]{2,1,0:T(8,128)}, u32[]{:S(2)}) copy-start(f32[1,64,2048]{2,1,0:T(8,128)} %dw_ref.1) | copy-start | bytes 1572868
  0.7 97.6 %copy-start.5 = (f32[1,64,256]{2,1,0:T(8,128)S(1)}, f32[1,64,256]{2,1,0:T(8,128)}, u32[]{:S(2)}) copy-start(f32[1,64,256]{2,1,0:T(8,128)} %param.18) | copy-start | bytes 196612
  0.7 97.6 %copy-start.4 = (f32[1,64,256]{2,1,0:T(8,128)S(1)}, f32[1,64,256]{2,1,0:T(8,128)}, u32[]{:S(2)}) copy-start(f32[1,64,256]{2,1,0:T(8,128)} %param.17) | copy-start | bytes 196612
  0.7 99.1 %copy-start.2 = (f32[1,64,2048]{2,1,0:T(8,128)S(1)}, f32[1,64,2048]{2,1,0:T(8,128)}, u32[]{:S(2)}) copy-start(f32[1,64,2048]{2,1,0:T(8,128)} %param.16) | copy-start | bytes 1572868
  0.7 99.1 %copy-start.1 = (f32[1,64,2048]{2,1,0:T(8,128)S(1)}, f32[1,64,2048]{2,1,0:T(8,128)}, u32[]{:S(2)}) copy-start(f32[1,64,2048]{2,1,0:T(8,128)} %param.15) | copy-start | bytes 1572868

commit v3 on v2

--- a/solution.py
+++ b/solution.py
@@ -187,7 +187,9 @@
     prec,
     own_base,
     bpart,
+    bpair,
     lpart,
+    lpair,
     back_half,
     low_half,
     acc,
@@ -304,13 +306,17 @@
         )
 
     def copy_b(k):
-        return remote(
-            bpart.at[0], bpart.at[k], send_b.at[k - 1], recv_b.at[k - 1], owner=mod(own + k)
+        flip = 1 - 2 * lax.rem(own, 2) if k == 1 else 2 - 4 * (own // 2)
+        part = bpart if k == 1 else bpair
+        return remote(
+            part.at[0], part.at[1], send_b.at[k - 1], recv_b.at[k - 1], owner=own + flip
         )
 
     def copy_l(k):
-        return remote(
-            lpart.at[0], lpart.at[k], send_l.at[k - 1], recv_l.at[k - 1], owner=mod(own + k)
+        flip = 1 - 2 * lax.rem(own, 2) if k == 1 else 2 - 4 * (own // 2)
+        part = lpart if k == 1 else lpair
+        return remote(
+            part.at[0], part.at[1], send_l.at[k - 1], recv_l.at[k - 1], owner=own + flip
         )
 
     def copy_c(k):
@@ -318,6 +324,14 @@
         return remote(
             csend.at[to], crecv.at[k - 1], send_c.at[k - 1], recv_c.at[k - 1], fsdp=to
         )
+
+    def start_c(stage):
+        for k in range(1, N):
+            to = mod(z + k)
+
+            @pl.when(jnp.where(to > z, to, N - 1 - to) == stage)
+            def _():
+                copy_c(k).start()
 
     def copy_e(k):
         to = mod(z + k)
@@ -415,23 +429,22 @@
         part = lax.dot_general(
             uall[owner_of(b)], g_ref[block_rows(b), :], NT, preferred_element_type=f32
         )
-        bpart[0, b] = (part * up_factor).astype(bf)
-
-    for k in range(1, N):
-        copy_b(k).start()
+        bpart[0, b] = part * up_factor
+
+    copy_b(1).start()
+    copy_b(1).wait_recv()
+    bpair[0] = (bpart[0] + bpart[1]).astype(bf)
+    copy_b(2).start()
     load_x.wait()
     product(z, True)
     forward(1, 0)
     send_own(2)
     product(z, False)
-    for k in range(1, N):
-        copy_b(k).wait_recv()
+    copy_b(2).wait_recv()
 
     @pl.loop(0, blocks)
     def _(b):
-        total = (bpart[0, b].astype(f32) + bpart[1, b].astype(f32)) + (
-            bpart[2, b].astype(f32) + bpart[3, b].astype(f32)
-        )
+        total = bpair[0, b].astype(f32) + bpair[1, b].astype(f32)
         back_half[b] = total.astype(bf)
 
     @pl.loop(0, width // COL_STEP)
@@ -451,6 +464,7 @@
 
     for f in range(N):
         csend[f] = acc[position_of(f)]
+    start_c(1)
 
     forward(2, 0)
     forward(1, 1)
@@ -463,21 +477,29 @@
         part = lax.dot_general(
             dall[owner_of(b)], x_ref[block_rows(b), :], NT, preferred_element_type=f32
         )
-        lpart[0, b] = (part * down_factor).astype(bf)
-
-    for k in range(1, N):
-        copy_l(k).start()
+        lpart[0, b] = part * down_factor
+
+    copy_l(1).start()
+    copy_l(1).wait_recv()
+    lpair[0] = (lpart[0] + lpart[1]).astype(bf)
+    copy_l(2).start()
     forward(2, 2)
+    start_c(2)
     line_products(2)
     cross_products(1)
-    for k in range(1, N):
-        copy_l(k).wait_recv()
+    cross_products(2)
+    forward(3, 1)
+    forward(3, 2)
+    for kind in (1, 2):
+        sent_forward(2, kind)
+    start_c(3)
+    line_products(3)
+    cross_products(3)
+    copy_l(2).wait_recv()
 
     @pl.loop(0, blocks)
     def _(b):
-        total = (lpart[0, b].astype(f32) + lpart[1, b].astype(f32)) + (
-            lpart[2, b].astype(f32) + lpart[3, b].astype(f32)
-        )
+        total = lpair[0, b].astype(f32) + lpair[1, b].astype(f32)
         half = total.astype(bf)
         low_half[b] = half
         extra[block_rows(b), :] = up_factor * lax.dot_general(
@@ -499,15 +521,6 @@
         esend[f] = acc[position_of(f), :, 0:256]
     for k in range(1, N):
         copy_e(k).start()
-    forward(3, 1)
-    forward(3, 2)
-    for kind in (1, 2):
-        sent_forward(2, kind)
-    for k in range(1, N):
-        copy_c(k).start()
-    line_products(3)
-    cross_products(2)
-    cross_products(3)
 
     for k in range(1, N):
         copy_e(k).wait_recv()
@@ -541,8 +554,10 @@
 
     for k in range(1, N):
         copy_a(k).wait_send()
-        copy_b(k).wait_send()
-        copy_l(k).wait_send()
+        if k < 3:
+            copy_b(k).wait_send()
+        if k < 3:
+            copy_l(k).wait_send()
         copy_c(k).wait_send()
         copy_e(k).wait_send()
     for kind in range(3):
@@ -603,8 +618,10 @@
             pltpu.VMEM((N, 2, tokens, HALF), bf),
             pltpu.VMEM((2, 3, tokens, HALF), bf),
             pltpu.VMEM((2, tokens, HALF), f32),
-            pltpu.VMEM((N, blocks, RANK, BLOCK), bf),
-            pltpu.VMEM((N, blocks, RANK, BLOCK), bf),
+            pltpu.VMEM((2, blocks, RANK, BLOCK), f32),
+            pltpu.VMEM((2, blocks, RANK, BLOCK), bf),
+            pltpu.VMEM((2, blocks, RANK, BLOCK), f32),
+            pltpu.VMEM((2, blocks, RANK, BLOCK), bf),
             pltpu.VMEM((blocks, RANK, BLOCK), bf),
             pltpu.VMEM((blocks, RANK, BLOCK), bf),
             pltpu.VMEM((N, RANK, width), bf),

time: 103 us -> 100 us (0.971)
  Pallas kernels: 95.1 us -> 92.8 us
    pallas_call x1, Pallas kernels: 95.1 us -> 92.8 us  [per_device_fused(): pl.pallas_call(fused_kernel, out_shape=(jax.ShapeDtypeStruct((tokens, 256...]
where the time goes in v3:
time: 100 us; the launch traced here: 99.9 us
  Pallas kernels  92.8 us (93%)
  other arithmetic  6.41 us (6%)
    pallas_call x1, Pallas kernels, per_device_fused(): pl.pallas_call(fused_kernel, out_shape=(jax.ShapeDtypeStruct((tokens, 256...  92.8 us
    sub x2, other arithmetic, adam_weight_update(): new_weights = weights - learning_rate * (direction + decay_rate * weights)  3.97 us
    convert_element_type x1, other arithmetic, per_device_fused(): return (values.astype(bf), ndw, nuw, ndm, nds, num, nus)  2.44 us

profile of v3, /device:TPU:7, one launch (start us, length us, event | category | flops | bytes accessed | tf_op | source)
XLA Modules:
  0.0 99.9 jit_solution(7876475393494561461)
XLA Ops:
  0.6 0.0 copy-start.3
  0.6 0.0 copy-start
  0.7 0.0 copy-start.5
  0.7 0.0 copy-start.4
  0.7 0.0 copy-start.2
  0.7 0.0 copy-start.1
  0.7 92.8 %shard_map.162 = (f32[1664,256]{1,0:T(8,128)}, f32[1,64,2048]{2,1,0:T(8,128)}, f32[1,64,256]{2,1,0:T(8,128)}) custom-call(s32[52]{0:T(128)} %tenant_ref.1, s32[4]{0:T(128)} %storage_ref.1, bf16[1664,2048]{1,0:T(8,128)(2,1)} %x_hbm.1, bf16[256,2048]{1,0:T(8,128)(2,1)} %v_ref.1, f32[1,64,2048]{2,1,0:T(8,128)} %dw_ref.1, f32[1,64,256]{2,1,0:T(8,128)} %uw_ref.1, ...), custom_call_target="tpu_custom_call" | custom-call | tf_op jit(solution)/shard_map/pallas_call | solution.py:602
  93.5 2.4 %convert_element_type.3 = bf16[1664,256]{1,0:T(8,128)(2,1)} convert(f32[1664,256]{1,0:T(8,128)} %get-tuple-element.10) | non-fusion elementwise | flops 425984 | bytes 2555904 | tf_op jit(solution)/shard_map/convert_element_type | solution.py:669
  95.9 0.0 copy-done.3
  95.9 0.0 copy-done.5
  95.9 0.0 copy-done.4
  95.9 1.5 %multiply_subtract_fusion.1 = (f32[1,64,256]{2,1,0:T(8,128)}, f32[1,64,256]{2,1,0:T(8,128)}, f32[1,64,256]{2,1,0:T(8,128)}) fusion(f32[1,64,256]{2,1,0:T(8,128)S(1)} %copy-done.3, f32[1,64,256]{2,1,0:T(8,128)} %get-tuple-element.12, f32[1,64,256]{2,1,0:T(8,128)S(1)} %copy-done.4, f32[1,64,256]{2,1,0:T(8,128)S(1)} %copy-done.5), kind=kLoop, calls=%fused_computation.6 | loop fusion | flops 245760 | bytes 458752 | tf_op jit(solution)/shard_map/sub | solution.py:28
  97.5 0.0 copy-done
  97.5 0.0 copy-done.2
  97.5 0.0 copy-done.1
  97.5 2.4 %multiply_subtract_fusion = (f32[1,64,2048]{2,1,0:T(8,128)}, f32[1,64,2048]{2,1,0:T(8,128)}, f32[1,64,2048]{2,1,0:T(8,128)}) fusion(f32[1,64,2048]{2,1,0:T(8,128)S(1)} %copy-done, f32[1,64,2048]{2,1,0:T(8,128)} %get-tuple-element.11, f32[1,64,2048]{2,1,0:T(8,128)S(1)} %copy-done.1, f32[1,64,2048]{2,1,0:T(8,128)S(1)} %copy-done.2), kind=kLoop, calls=%fused_computation.2 | loop fusion | flops 1966080 | bytes 3670016 | tf_op jit(solution)/shard_map/sub | solution.py:28
Async XLA Ops:
  0.6 95.3 %copy-start.3 = (f32[1,64,256]{2,1,0:T(8,128)S(1)}, f32[1,64,256]{2,1,0:T(8,128)}, u32[]{:S(2)}) copy-start(f32[1,64,256]{2,1,0:T(8,128)} %uw_ref.1) | copy-start | bytes 196612
  0.6 96.8 %copy-start = (f32[1,64,2048]{2,1,0:T(8,128)S(1)}, f32[1,64,2048]{2,1,0:T(8,128)}, u32[]{:S(2)}) copy-start(f32[1,64,2048]{2,1,0:T(8,128)} %dw_ref.1) | copy-start | bytes 1572868
  0.7 95.3 %copy-start.5 = (f32[1,64,256]{2,1,0:T(8,128)S(1)}, f32[1,64,256]{2,1,0:T(8,128)}, u32[]{:S(2)}) copy-start(f32[1,64,256]{2,1,0:T(8,128)} %param.18) | copy-start | bytes 196612
  0.7 95.3 %copy-start.4 = (f32[1,64,256]{2,1,0:T(8,128)S(1)}, f32[1,64,256]{2,1,0:T(8,128)}, u32[]{:S(2)}) copy-start(f32[1,64,256]{2,1,0:T(8,128)} %param.17) | copy-start | bytes 196612
  0.7 96.8 %copy-start.2 = (f32[1,64,2048]{2,1,0:T(8,128)S(1)}, f32[1,64,2048]{2,1,0:T(8,128)}, u32[]{:S(2)}) copy-start(f32[1,64,2048]{2,1,0:T(8,128)} %param.16) | copy-start | bytes 1572868
  0.7 96.8 %copy-start.1 = (f32[1,64,2048]{2,1,0:T(8,128)S(1)}, f32[1,64,2048]{2,1,0:T(8,128)}, u32[]{:S(2)}) copy-start(f32[1,64,2048]{2,1,0:T(8,128)} %param.15) | copy-start | bytes 1572868
